TPU v7x, 32 devices: a whole 2x2x4 slice. The times are simulated.
32 devices in a mesh: month: 4 (over y, x), grid: 8 (over z, core).
Axes of the slice: x: 2, y: 2, z: 4, core: 2. Of those that a mesh axis runs over, the one named last changes fastest.
Arguments:
- tracers: float32 [64, 8192], P(None, 'grid'), may hold values from 0.25 to 7
- targets: float32 [64], replicated, may hold values from 0.5 to 2
- retain: float32 [8, 8192], P('month', 'grid'), may hold values from 0.5 to 0.95
- blocks: float32 [8, 64, 8, 128, 128], P('month', 'grid'), may hold values from 3.90625e-07 to 0.00390625
- cols: int32 [8, 64, 8], P('month', 'grid'), may hold values from 0 to 63, as said below
Outputs:
- spun_up: float32 [64, 8192], P('month', 'grid')
Inputs may be any that keep to these rules, and one draw needn't show every extreme that they name: cols[m, i, 0] = i; for 1 <= k < 6, cols[m, i, k] names a block on the same grid device as block i (block b lies on device b // 8); the last 2 entries name blocks on other devices, and of the 16 such entries of one device's block rows in one month at most 3 lie on any single device, exactly 3 on some.
All inputs are finite; a program needn't handle non-finite values.
Results may differ from a plain program's by a relative error of at most 0.0001.
Values sent between devices are 32-bit elements; how exact they have to be, the bound alone decides.
A program may use at most 64 MiB of HBM per device.

v0:
```python
import jax
import jax.numpy as jnp
from jax import lax
from jax.sharding import PartitionSpec as P


def passed_along(value, axis, by):
    devices = lax.axis_size(axis)
    return lax.ppermute(value, axis, [(i, (i + by) % devices) for i in range(devices)])


def local(tracers, targets, retain, blocks, cols):
    sections = lax.axis_size("month")
    devices = lax.axis_size("grid")
    section = lax.axis_index("month")
    months_here = blocks.shape[0]
    blk_count = blocks.shape[1]
    blk_size = blocks.shape[3]
    rows_here = blk_count * blk_size
    batch = tracers.shape[0] // sections
    points = rows_here * devices
    held = jnp.zeros((batch, rows_here), jnp.float32)
    kept = jnp.zeros((batch, rows_here), jnp.float32)
    last_step = max(2 * sections - 2, 3 * sections - 4)
    for step in range(last_step + 1):
        if step < sections:
            held = jnp.where(section == 0, tracers[step * batch : (step + 1) * batch], held)
        if step < 2 * sections - 1:
            working = (step - section >= 0) & (step - section < sections)
            apply_state = held
            for apply_month_idx in range(months_here):
                whole = lax.all_gather(apply_state, "grid", axis=1, tiled=True)
                picked = whole.reshape(batch, -1, blk_size)[:, cols[apply_month_idx]]
                mixed = jnp.einsum(
                    "tbkc,bkrc->tbr",
                    picked,
                    blocks[apply_month_idx],
                    precision=lax.Precision.HIGHEST,
                    preferred_element_type=jnp.float32,
                )
                apply_state = retain[apply_month_idx][None, :] * apply_state + mixed.reshape(
                    batch, rows_here
                )
            held = jnp.where(working, apply_state, held)
            finished = step - sections + 1
            if finished >= 0:
                inventory = lax.psum(jnp.sum(held, axis=1), "grid")
                goal = targets[finished * batch : (finished + 1) * batch]
                scaled = held * (goal * points / inventory)[:, None]
                held = jnp.where(section == sections - 1, scaled, held)
        arrived = jnp.where(
            section == sections - 1, step == 2 * sections - 2, step == sections + 2 * section
        )
        kept = jnp.where(arrived, held, kept)
        if step < last_step:
            held = passed_along(held, "month", 1)
    return kept


def solution(mesh):
    return jax.shard_map(
        local,
        mesh=mesh,
        in_specs=(
            P(None, "grid"),
            P(),
            P("month", "grid"),
            P("month", "grid", None, None, None),
            P("month", "grid", None),
        ),
        out_specs=P("month", "grid"),
        check_vma=False,
    )
```

profile of v0, /device:TPU:6, one launch (start us, length us, event | category | flops | bytes accessed | tf_op | source)
XLA Modules:
  0.0 398.8 jit_solution(2094131515093667880)
XLA Ops:
  0.9 15.1 %all_gather.42 = f32[16,8192]{1,0:T(8,128)S(1)} all-gather(f32[16,1024]{1,0:T(8,128)S(1)} %slice_select_fusion), channel_id=1, replica_groups=mesh['month'=4,'grid'=8] {'grid'}, dimensions={1}, use_global_device_ids=true | all-gather | bytes 589824 | tf_op jit(solution)/shard_map/all_gather | solution.py:32
  18.3 5.3 %fusion.42 = f32[8,2,8,128]{3,2,1,0:T(8,128)S(1)} fusion(f32[16,8,8,128]{3,0,2,1:T(8,128)S(1)} %bitcast.326, f32[2,8,8,128,128]{4,3,2,1,0:T(8,128)} %param.8), kind=kOutput, calls=%fused_computation.56 | convolution fusion | flops 201326592 | bytes 4784128 | tf_op jit(solution)/shard_map/tbkc,bkrc->tbr/dot_general | solution.py:34
  24.5 14.7 %all_gather.43 = f32[16,8192]{1,0:T(8,128)S(1)} all-gather(f32[16,1024]{1,0:T(8,128)S(1)} %bitcast_add_fusion.13), channel_id=1, replica_groups=mesh['month'=4,'grid'=8] {'grid'}, dimensions={1}, use_global_device_ids=true | all-gather | bytes 589824 | tf_op jit(solution)/shard_map/all_gather | solution.py:32
  40.0 5.3 %fusion.63 = f32[8,2,8,128]{3,2,1,0:T(8,128)S(1)} fusion(f32[16,8,8,128]{3,0,2,1:T(8,128)S(1)} %bitcast.327, f32[2,8,8,128,128]{4,3,2,1,0:T(8,128)} %param.8), kind=kOutput, calls=%fused_computation.63 | convolution fusion | flops 201326592 | bytes 4784128 | tf_op jit(solution)/shard_map/tbkc,bkrc->tbr/dot_general | solution.py:34
  49.7 15.1 %all_gather.44 = f32[16,8192]{1,0:T(8,128)S(1)} all-gather(f32[16,1024]{1,0:T(8,128)S(1)} %slice_select_fusion.1), channel_id=1, replica_groups=mesh['month'=4,'grid'=8] {'grid'}, dimensions={1}, use_global_device_ids=true | all-gather | bytes 589824 | tf_op jit(solution)/shard_map/all_gather | solution.py:32
  65.5 5.3 %fusion.45 = f32[8,2,8,128]{3,2,1,0:T(8,128)S(1)} fusion(f32[16,8,8,128]{3,0,2,1:T(8,128)S(1)} %bitcast.328, f32[2,8,8,128,128]{4,3,2,1,0:T(8,128)} %param.8), kind=kOutput, calls=%fused_computation.57 | convolution fusion | flops 201326592 | bytes 4784128 | tf_op jit(solution)/shard_map/tbkc,bkrc->tbr/dot_general | solution.py:34
  70.8 15.1 %all_gather.45 = f32[16,8192]{1,0:T(8,128)S(1)} all-gather(f32[16,1024]{1,0:T(8,128)S(1)} %bitcast_add_fusion.11), channel_id=1, replica_groups=mesh['month'=4,'grid'=8] {'grid'}, dimensions={1}, use_global_device_ids=true | all-gather | bytes 589824 | tf_op jit(solution)/shard_map/all_gather | solution.py:32
  86.6 5.3 %fusion.66 = f32[8,2,8,128]{3,2,1,0:T(8,128)S(1)} fusion(f32[16,8,8,128]{3,0,2,1:T(8,128)S(1)} %bitcast.329, f32[2,8,8,128,128]{4,3,2,1,0:T(8,128)} %param.8), kind=kOutput, calls=%fused_computation.64 | convolution fusion | flops 201326592 | bytes 4784128 | tf_op jit(solution)/shard_map/tbkc,bkrc->tbr/dot_general | solution.py:34
  96.3 15.4 %all_gather.46 = f32[16,8192]{1,0:T(8,128)S(1)} all-gather(f32[16,1024]{1,0:T(8,128)S(1)} %slice_select_fusion.2), channel_id=1, replica_groups=mesh['month'=4,'grid'=8] {'grid'}, dimensions={1}, use_global_device_ids=true | all-gather | bytes 589824 | tf_op jit(solution)/shard_map/all_gather | solution.py:32
  112.3 5.3 %fusion.48 = f32[8,2,8,128]{3,2,1,0:T(8,128)S(1)} fusion(f32[16,8,8,128]{3,0,2,1:T(8,128)S(1)} %bitcast.330, f32[2,8,8,128,128]{4,3,2,1,0:T(8,128)} %param.8), kind=kOutput, calls=%fused_computation.58 | convolution fusion | flops 201326592 | bytes 4784128 | tf_op jit(solution)/shard_map/tbkc,bkrc->tbr/dot_general | solution.py:34
  117.7 15.1 %all_gather.47 = f32[16,8192]{1,0:T(8,128)S(1)} all-gather(f32[16,1024]{1,0:T(8,128)S(1)} %bitcast_add_fusion.9), channel_id=1, replica_groups=mesh['month'=4,'grid'=8] {'grid'}, dimensions={1}, use_global_device_ids=true | all-gather | bytes 589824 | tf_op jit(solution)/shard_map/all_gather | solution.py:32
  133.4 5.3 %fusion.69 = f32[8,2,8,128]{3,2,1,0:T(8,128)S(1)} fusion(f32[16,8,8,128]{3,0,2,1:T(8,128)S(1)} %bitcast.331, f32[2,8,8,128,128]{4,3,2,1,0:T(8,128)} %param.8), kind=kOutput, calls=%fused_computation.65 | convolution fusion | flops 201326592 | bytes 4784128 | tf_op jit(solution)/shard_map/tbkc,bkrc->tbr/dot_general | solution.py:34
  143.7 15.2 %all_gather.48 = f32[16,8192]{1,0:T(8,128)S(1)} all-gather(f32[16,1024]{1,0:T(8,128)S(1)} %slice_select_fusion.3), channel_id=1, replica_groups=mesh['month'=4,'grid'=8] {'grid'}, dimensions={1}, use_global_device_ids=true | all-gather | bytes 589824 | tf_op jit(solution)/shard_map/all_gather | solution.py:32
  159.6 5.3 %fusion.51 = f32[8,2,8,128]{3,2,1,0:T(8,128)S(1)} fusion(f32[16,8,8,128]{3,0,2,1:T(8,128)S(1)} %bitcast.332, f32[2,8,8,128,128]{4,3,2,1,0:T(8,128)} %param.8), kind=kOutput, calls=%fused_computation.59 | convolution fusion | flops 201326592 | bytes 4784128 | tf_op jit(solution)/shard_map/tbkc,bkrc->tbr/dot_general | solution.py:34
  164.9 15.0 %all_gather.49 = f32[16,8192]{1,0:T(8,128)S(1)} all-gather(f32[16,1024]{1,0:T(8,128)S(1)} %bitcast_add_fusion.7), channel_id=1, replica_groups=mesh['month'=4,'grid'=8] {'grid'}, dimensions={1}, use_global_device_ids=true | all-gather | bytes 589824 | tf_op jit(solution)/shard_map/all_gather | solution.py:32
  180.6 5.3 %fusion.72 = f32[8,2,8,128]{3,2,1,0:T(8,128)S(1)} fusion(f32[16,8,8,128]{3,0,2,1:T(8,128)S(1)} %bitcast.333, f32[2,8,8,128,128]{4,3,2,1,0:T(8,128)} %param.8), kind=kOutput, calls=%fused_computation.66 | convolution fusion | flops 201326592 | bytes 4784128 | tf_op jit(solution)/shard_map/tbkc,bkrc->tbr/dot_general | solution.py:34
  186.0 17.3 %psum.28 = f32[16]{0:T(128)S(1)} all-reduce(f32[16]{0:T(128)S(1)} %get-tuple-element.11), channel_id=1, replica_groups=mesh['month'=4,'grid'=8] {'grid'}, use_global_device_ids=true, to_apply=%region_1.2 | all-reduce | flops 16 | bytes 128 | tf_op jit(solution)/shard_map/psum | solution.py:47
  208.4 15.2 %all_gather.50 = f32[16,8192]{1,0:T(8,128)S(1)} all-gather(f32[16,1024]{1,0:T(8,128)S(1)} %collective-permute-done.3), channel_id=1, replica_groups=mesh['month'=4,'grid'=8] {'grid'}, dimensions={1}, use_global_device_ids=true | all-gather | bytes 589824 | tf_op jit(solution)/shard_map/all_gather | solution.py:32
  224.3 5.3 %fusion.54 = f32[8,2,8,128]{3,2,1,0:T(8,128)S(1)} fusion(f32[16,8,8,128]{3,0,2,1:T(8,128)S(1)} %bitcast.334, f32[2,8,8,128,128]{4,3,2,1,0:T(8,128)} %param.8), kind=kOutput, calls=%fused_computation.60 | convolution fusion | flops 201326592 | bytes 4784128 | tf_op jit(solution)/shard_map/tbkc,bkrc->tbr/dot_general | solution.py:34
  229.6 15.0 %all_gather.51 = f32[16,8192]{1,0:T(8,128)S(1)} all-gather(f32[16,1024]{1,0:T(8,128)S(1)} %bitcast_add_fusion.5), channel_id=1, replica_groups=mesh['month'=4,'grid'=8] {'grid'}, dimensions={1}, use_global_device_ids=true | all-gather | bytes 589824 | tf_op jit(solution)/shard_map/all_gather | solution.py:32
  245.3 5.3 %fusion.75 = f32[8,2,8,128]{3,2,1,0:T(8,128)S(1)} fusion(f32[16,8,8,128]{3,0,2,1:T(8,128)S(1)} %bitcast.335, f32[2,8,8,128,128]{4,3,2,1,0:T(8,128)} %param.8), kind=kOutput, calls=%fused_computation.67 | convolution fusion | flops 201326592 | bytes 4784128 | tf_op jit(solution)/shard_map/tbkc,bkrc->tbr/dot_general | solution.py:34
  250.7 13.9 %psum.29 = f32[16]{0:T(128)S(1)} all-reduce(f32[16]{0:T(128)S(1)} %get-tuple-element.9), channel_id=1, replica_groups=mesh['month'=4,'grid'=8] {'grid'}, use_global_device_ids=true, to_apply=%region_3.4 | all-reduce | flops 16 | bytes 128 | tf_op jit(solution)/shard_map/psum | solution.py:47
  270.0 15.0 %all_gather.52 = f32[16,8192]{1,0:T(8,128)S(1)} all-gather(f32[16,1024]{1,0:T(8,128)S(1)} %collective-permute-done.4), channel_id=1, replica_groups=mesh['month'=4,'grid'=8] {'grid'}, dimensions={1}, use_global_device_ids=true | all-gather | bytes 589824 | tf_op jit(solution)/shard_map/all_gather | solution.py:32
  285.6 5.3 %fusion.57 = f32[8,2,8,128]{3,2,1,0:T(8,128)S(1)} fusion(f32[16,8,8,128]{3,0,2,1:T(8,128)S(1)} %bitcast.336, f32[2,8,8,128,128]{4,3,2,1,0:T(8,128)} %param.8), kind=kOutput, calls=%fused_computation.61 | convolution fusion | flops 201326592 | bytes 4784128 | tf_op jit(solution)/shard_map/tbkc,bkrc->tbr/dot_general | solution.py:34
  291.0 15.0 %all_gather.53 = f32[16,8192]{1,0:T(8,128)S(1)} all-gather(f32[16,1024]{1,0:T(8,128)S(1)} %bitcast_add_fusion.3), channel_id=1, replica_groups=mesh['month'=4,'grid'=8] {'grid'}, dimensions={1}, use_global_device_ids=true | all-gather | bytes 589824 | tf_op jit(solution)/shard_map/all_gather | solution.py:32
  306.6 5.3 %fusion.78 = f32[8,2,8,128]{3,2,1,0:T(8,128)S(1)} fusion(f32[16,8,8,128]{3,0,2,1:T(8,128)S(1)} %bitcast.337, f32[2,8,8,128,128]{4,3,2,1,0:T(8,128)} %param.8), kind=kOutput, calls=%fused_computation.68 | convolution fusion | flops 201326592 | bytes 4784128 | tf_op jit(solution)/shard_map/tbkc,bkrc->tbr/dot_general | solution.py:34
  312.1 13.9 %psum.30 = f32[16]{0:T(128)S(1)} all-reduce(f32[16]{0:T(128)S(1)} %get-tuple-element.7), channel_id=1, replica_groups=mesh['month'=4,'grid'=8] {'grid'}, use_global_device_ids=true, to_apply=%region_5.6 | all-reduce | flops 16 | bytes 128 | tf_op jit(solution)/shard_map/psum | solution.py:47
  331.3 15.3 %all_gather.54 = f32[16,8192]{1,0:T(8,128)S(1)} all-gather(f32[16,1024]{1,0:T(8,128)S(1)} %collective-permute-done.5), channel_id=1, replica_groups=mesh['month'=4,'grid'=8] {'grid'}, dimensions={1}, use_global_device_ids=true | all-gather | bytes 589824 | tf_op jit(solution)/shard_map/all_gather | solution.py:32
  347.3 5.3 %fusion.60 = f32[8,2,8,128]{3,2,1,0:T(8,128)S(1)} fusion(f32[16,8,8,128]{3,0,2,1:T(8,128)S(1)} %bitcast.324, f32[2,8,8,128,128]{4,3,2,1,0:T(8,128)} %param.8), kind=kOutput, calls=%fused_computation.62 | convolution fusion | flops 201326592 | bytes 4784128 | tf_op jit(solution)/shard_map/tbkc,bkrc->tbr/dot_general | solution.py:34
  352.6 15.0 %all_gather.55 = f32[16,8192]{1,0:T(8,128)S(1)} all-gather(f32[16,1024]{1,0:T(8,128)S(1)} %bitcast_add_fusion.1), channel_id=1, replica_groups=mesh['month'=4,'grid'=8] {'grid'}, dimensions={1}, use_global_device_ids=true | all-gather | bytes 589824 | tf_op jit(solution)/shard_map/all_gather | solution.py:32
  368.3 5.3 %fusion.81 = f32[8,2,8,128]{3,2,1,0:T(8,128)S(1)} fusion(f32[16,8,8,128]{3,0,2,1:T(8,128)S(1)} %bitcast.325, f32[2,8,8,128,128]{4,3,2,1,0:T(8,128)} %param.8), kind=kOutput, calls=%fused_computation.69 | convolution fusion | flops 201326592 | bytes 4784128 | tf_op jit(solution)/shard_map/tbkc,bkrc->tbr/dot_general | solution.py:34
  373.7 13.9 %psum.31 = f32[16]{0:T(128)S(1)} all-reduce(f32[16]{0:T(128)S(1)} %get-tuple-element.5), channel_id=1, replica_groups=mesh['month'=4,'grid'=8] {'grid'}, use_global_device_ids=true, to_apply=%region_7.8 | all-reduce | flops 16 | bytes 128 | tf_op jit(solution)/shard_map/psum | solution.py:47
  (81 shorter events, 54.2 us)
Async XLA Ops:
  0.0 45.3 %copy-start = (f32[64,1024]{1,0:T(8,128)S(1)}, f32[64,1024]{1,0:T(8,128)}, u32[]{:S(2)}) copy-start(f32[64,1024]{1,0:T(8,128)} %param.5) | copy-start | bytes 786436
  45.3 4.4 %collective-permute-start = (f32[16,1024]{1,0:T(8,128)S(1)}, f32[16,1024]{1,0:T(8,128)S(1)}, u32[]{:S(2)}, u32[]{:S(2)}) collective-permute-start(f32[16,1024]{1,0:T(8,128)S(1)} %fusion.90), channel_id=1, source_target_pairs={{0,8},{8,16},{16,24},{24,0},{1,9},{9,17},{17,25},{25,1},{2,10},{10... | collective-permute-start | bytes 196616 | tf_op jit(solution)/shard_map/ppermute | solution.py:9
  91.9 4.4 %collective-permute-start.1 = (f32[16,1024]{1,0:T(8,128)S(1)}, f32[16,1024]{1,0:T(8,128)S(1)}, u32[]{:S(2)}, u32[]{:S(2)}) collective-permute-start(f32[16,1024]{1,0:T(8,128)S(1)} %fusion.89), channel_id=1, source_target_pairs={{0,8},{8,16},{16,24},{24,0},{1,9},{9,17},{17,25},{25,1},{2,10},{10... | collective-permute-start | bytes 196616 | tf_op jit(solution)/shard_map/ppermute | solution.py:9
  138.7 64.7 %copy-start.1 = (f32[64]{0:T(128)S(1)}, f32[64]{0:T(128)}, u32[]{:S(2)}) copy-start(f32[64]{0:T(128)} %param.6) | copy-start | bytes 772
  138.7 5.0 %collective-permute-start.2 = (f32[16,1024]{1,0:T(8,128)S(1)}, f32[16,1024]{1,0:T(8,128)S(1)}, u32[]{:S(2)}, u32[]{:S(2)}) collective-permute-start(f32[16,1024]{1,0:T(8,128)S(1)} %fusion.88), channel_id=1, source_target_pairs={{0,8},{8,16},{16,24},{24,0},{1,9},{9,17},{17,25},{25,1},{2,10},{10... | collective-permute-start | bytes 196616 | tf_op jit(solution)/shard_map/ppermute | solution.py:9
  203.4 5.0 %collective-permute-start.3 = (f32[16,1024]{1,0:T(8,128)S(1)}, f32[16,1024]{1,0:T(8,128)S(1)}, u32[]{:S(2)}, u32[]{:S(2)}) collective-permute-start(f32[16,1024]{1,0:T(8,128)S(1)} %multiply_select_fusion.3), channel_id=1, source_target_pairs={{0,8},{8,16},{16,24},{24,0},{1,9},{9,17},{17,25},{25,1},{2,10},{10... | collective-permute-start | bytes 196616 | tf_op jit(solution)/shard_map/ppermute | solution.py:9
  264.8 5.2 %collective-permute-start.4 = (f32[16,1024]{1,0:T(8,128)S(1)}, f32[16,1024]{1,0:T(8,128)S(1)}, u32[]{:S(2)}, u32[]{:S(2)}) collective-permute-start(f32[16,1024]{1,0:T(8,128)S(1)} %multiply_select_fusion.2), channel_id=1, source_target_pairs={{0,8},{8,16},{16,24},{24,0},{1,9},{9,17},{17,25},{25,1},{2,10},{10... | collective-permute-start | bytes 196616 | tf_op jit(solution)/shard_map/ppermute | solution.py:9
  326.1 5.2 %collective-permute-start.5 = (f32[16,1024]{1,0:T(8,128)S(1)}, f32[16,1024]{1,0:T(8,128)S(1)}, u32[]{:S(2)}, u32[]{:S(2)}) collective-permute-start(f32[16,1024]{1,0:T(8,128)S(1)} %multiply_select_fusion.1), channel_id=1, source_target_pairs={{0,8},{8,16},{16,24},{24,0},{1,9},{9,17},{17,25},{25,1},{2,10},{10... | collective-permute-start | bytes 196616 | tf_op jit(solution)/shard_map/ppermute | solution.py:9
  387.8 5.2 %collective-permute-start.6 = (f32[16,1024]{1,0:T(8,128)S(1)}, f32[16,1024]{1,0:T(8,128)S(1)}, u32[]{:S(2)}, u32[]{:S(2)}) collective-permute-start(f32[16,1024]{1,0:T(8,128)S(1)} %multiply_select_fusion), channel_id=1, source_target_pairs={{0,8},{8,16},{16,24},{24,0},{1,9},{9,17},{17,25},{25,1},{2,10},{10... | collective-permute-start | bytes 196616 | tf_op jit(solution)/shard_map/ppermute | solution.py:9
  392.9 5.2 %collective-permute-start.7 = (f32[16,1024]{1,0:T(8,128)S(1)}, f32[16,1024]{1,0:T(8,128)S(1)}, u32[]{:S(2)}, u32[]{:S(2)}) collective-permute-start(f32[16,1024]{1,0:T(8,128)S(1)} %collective-permute-done.6), channel_id=1, source_target_pairs={{0,8},{8,16},{16,24},{24,0},{1,9},{9,17},{17,25},{25,1},{2,10},{10... | collective-permute-start | bytes 196616 | tf_op jit(solution)/shard_map/ppermute | solution.py:9
where the time goes:
time: 403 us; the launch traced here: 399 us
  blocking collectives  270 us (67%)
  matrix products  74.1 us (18%)
  waiting for transfers between devices  21 us (5%)
  starting transfers between devices  18.4 us (5%)
  local copies, waits for them, and re-layouts  10.3 us (3%)
  other arithmetic  4.56 us (1%)
    all_gather x14, blocking collectives, local(): whole = lax.all_gather(apply_state, 'grid', axis=1, tiled=True)  211 us
    dot_general x14, matrix products, local(): jnp.einsum('tbkc,bkrc->tbr', picked, blocks[apply_month_idx], precision=l...  74.1 us
    psum x4, blocking collectives, local(): inventory = lax.psum(jnp.sum(held, axis=1), 'grid')  59.1 us
    ppermute x8, waiting for transfers between devices, passed_along(): lax.ppermute(value, axis, [(i, (i + by) % devices) for i in range(devices)])  21 us
    ppermute x8, starting transfers between devices, passed_along(): lax.ppermute(value, axis, [(i, (i + by) % devices) for i in range(devices)])  18.4 us
    gather x14, local copies, waits for them, and re-layouts, local(): picked = whole.reshape(batch, -1, blk_size)[:, cols[apply_month_idx]]  8.82 us
  transfers between devices with their start and end apart: 8, of which 8 were waited for; matrix products, arithmetic and copies ran while one was open for 0% of the time, Pallas kernels for 0%

commit v1 on v0

v1 whole, which is shorter than its diff:
```python
import functools

import jax
import jax.numpy as jnp
from jax import lax
from jax.experimental import pallas as pl
from jax.experimental.pallas import tpu as pltpu
from jax.sharding import PartitionSpec as P

FAR = 2
TB = 8
NT = (((1,), (1,)), ((), ()))
F32, BF16, I32 = jnp.float32, jnp.bfloat16, jnp.int32


def kernel(
    sections, n, cap, months, nb, kk, bs, nbatch,
    tracers, targets, retain, blocks, cols_s, cols_v,
    out,
    wf, whi, wlo, xin, xmid, xout, hl, cur, far, acc, sendbuf, recv, psend, precv, fout,
    cstage, crecv, csmem, send_tab, pos_tab,
    w_sem, c_send, c_recv, c_loc, h_send, h_recv, in_send, in_recv, p_send, p_recv, o_send, o_recv,
):
    tb = TB
    near = kk - FAR
    per = nbatch // sections
    last = sections - 1
    nfar = nb * FAR
    npts = float(n * nb * bs)
    s = lax.axis_index("month")
    g = lax.axis_index("grid")
    offsets = sorted(range(1, n), key=lambda o: abs(o - n // 2))

    def peer(o):
        return lax.rem(g + o, n)

    def chunk(j, i):
        return pltpu.make_async_copy(blocks.at[j, i], wf.at[j, i], w_sem.at[j, i])

    for j in range(months):
        for i in range(nb):
            chunk(j, i).start()

    barrier = pltpu.get_barrier_semaphore()
    for o in range(1, n):
        pl.semaphore_signal(barrier, inc=1, device_id={"grid": peer(o)}, device_id_type=pl.DeviceIdType.MESH)
    for o in range(1, sections):
        pl.semaphore_signal(
            barrier, inc=1, device_id={"month": lax.rem(s + o, sections)}, device_id_type=pl.DeviceIdType.MESH
        )
    cstage[...] = jnp.broadcast_to(cols_v[...], cstage.shape)
    pl.semaphore_wait(barrier, n - 1 + sections - 1)

    for o in offsets:
        pltpu.make_async_remote_copy(
            cstage, crecv.at[o - 1], c_send, c_recv,
            device_id={"grid": peer(o)}, device_id_type=pl.DeviceIdType.MESH,
        ).start()

    @pl.when(s == 0)
    def _():
        for b in range(nbatch):
            for i in range(nb):
                xin[b, i] = tracers[b * tb : (b + 1) * tb, i * bs : (i + 1) * bs]

    def far_at(j, e):
        return j * nb * kk + (e // FAR) * kk + near + e % FAR

    for j in range(months):
        owners = [cols_s[0, far_at(j, e)] // nb for e in range(nfar)]
        for e in range(nfar):
            rank = I32(0)
            for f in range(e):
                rank = rank + jnp.where(owners[f] == owners[e], 1, 0)
            off = g - owners[e]
            off = jnp.where(off < 0, off + n, off)
            pos_tab[j * nfar + e] = jnp.clip((off - 1) * cap + rank, 0, (n - 1) * cap - 1)

    pltpu.make_async_copy(crecv, crecv, c_recv).wait()
    local = pltpu.make_async_copy(crecv, csmem, c_loc)
    local.start()
    local.wait()

    def make_table(j):
        def one(q, carry):
            o = q + 1
            count = I32(0)
            idx = [I32(0)] * cap
            for e in range(nfar):
                c = csmem[n - 1 - o, 0, far_at(j, e)] - g * nb
                hit = (c >= 0) & (c < nb)
                for r in range(cap):
                    idx[r] = jnp.where(hit & (count == r), c, idx[r])
                count = count + jnp.where(hit, 1, 0)
            for r in range(cap):
                send_tab[(j * (n - 1) + q) * cap + r] = idx[r]
            return carry

        lax.fori_loop(0, n - 1, one, 0)

    def prep(j):
        def one(i, carry):
            chunk(j, i).wait()
            for k in range(kk):
                b = wf[j, i, k]
                hi = b.astype(BF16)
                whi[j, i, :, k * bs : (k + 1) * bs] = hi
                wlo[j, i, :, k * bs : (k + 1) * bs] = (b - hi.astype(F32)).astype(BF16)
            return carry

        lax.fori_loop(0, nb, one, 0)

    def split(v):
        hi = v.astype(BF16).astype(F32)
        return jnp.concatenate([hi, v - hi], axis=0).astype(BF16)

    def product(rows, j, i, lo, hi):
        d = lax.dot_general(rows, whi[j, i, :, lo * bs : hi * bs], NT, preferred_element_type=F32)
        d = d + lax.dot_general(rows, wlo[j, i, :, lo * bs : hi * bs], NT, preferred_element_type=F32)
        return d[:tb] + d[tb:]

    def send_halo(b, j, src):
        for i in range(nb):
            cur[i] = src[b, i]
        for o in offsets:
            for r in range(cap):
                q = (o - 1) * cap + r
                idx = send_tab[j * (n - 1) * cap + q]
                sendbuf[b, j, q] = cur[idx]
            pltpu.make_async_remote_copy(
                sendbuf.at[b, j, pl.ds((o - 1) * cap, cap)],
                recv.at[b, j, pl.ds((o - 1) * cap, cap)],
                h_send.at[b, j], h_recv.at[b, j],
                device_id={"grid": peer(o)}, device_id_type=pl.DeviceIdType.MESH,
            ).start()

    def apply(b, j, src, dst):
        for i in range(nb):
            hl[i] = split(src[b, i])
        for i in range(nb):
            picked = [hl[i]]
            for k in range(1, near):
                picked.append(hl[jnp.clip(cols_s[0, j * nb * kk + i * kk + k] - g * nb, 0, nb - 1)])
            rows = jnp.concatenate(picked, axis=1)
            keep = retain[j : j + 1, i * bs : (i + 1) * bs]
            acc[i] = keep * src[b, i] + product(rows, j, i, 0, near)
        pltpu.make_async_copy(recv.at[b, j], recv.at[b, j], h_recv.at[b, j]).wait()
        for q in range((n - 1) * cap):
            far[q] = split(recv[b, j, q])
        for i in range(nb):
            rows = jnp.concatenate([far[pos_tab[j * nfar + i * FAR + f]] for f in range(FAR)], axis=1)
            dst[b, i] = acc[i] + product(rows, j, i, near, kk)

    def enter(b):
        @pl.when(s > 0)
        def _():
            pltpu.make_async_copy(xin.at[b], xin.at[b], in_recv.at[b]).wait()

        send_halo(b, 0, xin)

    def middle(b):
        apply(b, 0, xin, xmid)
        send_halo(b, 1, xmid)

    def passed(b):
        return pltpu.make_async_remote_copy(
            xout.at[b], xin.at[b], in_send.at[b], in_recv.at[b],
            device_id={"month": lax.rem(s + 1, sections)}, device_id_type=pl.DeviceIdType.MESH,
        )

    def leave(b):
        apply(b, 1, xmid, xout)

        @pl.when(s < last)
        def _():
            passed(b).start()

        @pl.when(s == last)
        def _():
            total = xout[b, 0]
            for i in range(1, nb):
                total = total + xout[b, i]
            psend[b] = jnp.broadcast_to(jnp.sum(total, axis=1, keepdims=True), (tb, bs))
            for o in offsets:
                pltpu.make_async_remote_copy(
                    psend.at[b], precv.at[b, o - 1], p_send.at[b], p_recv.at[b],
                    device_id={"grid": peer(o)}, device_id_type=pl.DeviceIdType.MESH,
                ).start()

    def delivered(b):
        row = pl.multiple_of(lax.rem(b, per) * tb, tb)
        return pltpu.make_async_remote_copy(
            fout.at[b], out.at[pl.ds(row, tb)], o_send.at[b], o_recv,
            device_id={"month": lax.div(b, per)}, device_id_type=pl.DeviceIdType.MESH,
        )

    def finish(b):
        @pl.when(s == last)
        def _():
            pltpu.make_async_copy(precv.at[b], precv.at[b], p_recv.at[b]).wait()
            total = psend[b]
            for o in range(1, n):
                total = total + precv[b, o - 1]
            wide = jnp.broadcast_to(targets[...], (tb, targets.shape[1]))
            row = lax.broadcasted_iota(I32, wide.shape, 0) + b * tb
            col = lax.broadcasted_iota(I32, wide.shape, 1)
            goal = jnp.sum(jnp.where(row == col, wide, 0.0), axis=1, keepdims=True)
            factor = goal * npts / total
            for i in range(nb):
                fout[b, :, i * bs : (i + 1) * bs] = xout[b, i] * factor

            @pl.when(b < last * per)
            def _():
                delivered(b).start()

            @pl.when(b >= last * per)
            def _():
                at = pl.multiple_of(lax.rem(b, per) * tb, tb)
                out[pl.ds(at, tb), :] = fout[b]

    make_table(0)

    @pl.when(s == 0)
    def _():
        enter(I32(0))
        make_table(1)
        prep(0)

    @pl.when(s > 0)
    def _():
        make_table(1)
        prep(0)
        prep(1)
        enter(I32(0))

    middle(I32(0))

    @pl.when(s == 0)
    def _():
        prep(1)

    def step(b, carry):
        enter(b)
        leave(b - 1)
        middle(b)
        finish(b - 1)
        return carry

    lax.fori_loop(1, nbatch, step, 0)
    leave(I32(nbatch - 1))
    finish(I32(nbatch - 1))

    pltpu.make_async_copy(crecv, crecv, c_send).wait()

    def drain(b, carry):
        for j in range(months):
            pltpu.make_async_copy(sendbuf.at[b, j], sendbuf.at[b, j], h_send.at[b, j]).wait()

        @pl.when(s < last)
        def _():
            passed(b).wait_send()

        @pl.when(s == last)
        def _():
            pltpu.make_async_copy(precv.at[b], precv.at[b], p_send.at[b]).wait()

            @pl.when(b < last * per)
            def _():
                delivered(b).wait_send()

        return carry

    lax.fori_loop(0, nbatch, drain, 0)

    @pl.when(s < last)
    def _():
        pltpu.make_async_copy(out, out, o_recv).wait()


def solution(mesh):
    sections, n = mesh.shape["month"], mesh.shape["grid"]

    def local(tracers, targets, retain, blocks, cols):
        months, nb, kk, bs = blocks.shape[:4]
        count, rows = tracers.shape
        nbatch = count // TB
        cap = -(-nb * FAR // (n - 1))
        slots = (n - 1) * cap
        flat = cols.reshape(1, -1)
        dma = pltpu.SemaphoreType.DMA
        vmem = pl.BlockSpec(memory_space=pltpu.VMEM)
        return pl.pallas_call(
            functools.partial(kernel, sections, n, cap, months, nb, kk, bs, nbatch),
            out_shape=jax.ShapeDtypeStruct((count // sections, rows), F32),
            in_specs=[
                vmem, vmem, vmem,
                pl.BlockSpec(memory_space=pl.ANY),
                pl.BlockSpec(memory_space=pltpu.SMEM),
                vmem,
            ],
            out_specs=vmem,
            scratch_shapes=[
                pltpu.VMEM((months, nb, kk, bs, bs), F32),
                pltpu.VMEM((months, nb, bs, kk * bs), BF16),
                pltpu.VMEM((months, nb, bs, kk * bs), BF16),
                pltpu.VMEM((nbatch, nb, TB, bs), F32),
                pltpu.VMEM((nbatch, nb, TB, bs), F32),
                pltpu.VMEM((nbatch, nb, TB, bs), F32),
                pltpu.VMEM((nb, 2 * TB, bs), BF16),
                pltpu.VMEM((nb, TB, bs), F32),
                pltpu.VMEM((slots, 2 * TB, bs), BF16),
                pltpu.VMEM((nb, TB, bs), F32),
                pltpu.VMEM((nbatch, months, slots, TB, bs), F32),
                pltpu.VMEM((nbatch, months, slots, TB, bs), F32),
                pltpu.VMEM((nbatch, TB, bs), F32),
                pltpu.VMEM((nbatch, n - 1, TB, bs), F32),
                pltpu.VMEM((nbatch, TB, rows), F32),
                pltpu.VMEM((8, flat.shape[1]), I32),
                pltpu.VMEM((n - 1, 8, flat.shape[1]), I32),
                pltpu.SMEM((n - 1, 8, flat.shape[1]), I32),
                pltpu.SMEM((months * slots,), I32),
                pltpu.SMEM((months * nb * FAR,), I32),
                dma((months, nb)),
                dma, dma, dma,
                dma((nbatch, months)), dma((nbatch, months)),
                dma((nbatch,)), dma((nbatch,)),
                dma((nbatch,)), dma((nbatch,)),
                dma((nbatch,)), dma,
            ],
            compiler_params=pltpu.CompilerParams(
                collective_id=0, has_side_effects=True, vmem_limit_bytes=48 * 1024 * 1024
            ),
        )(tracers, targets.reshape(1, -1), retain, blocks, flat, flat)

    return jax.shard_map(
        local,
        mesh=mesh,
        in_specs=(
            P(None, "grid"),
            P(),
            P("month", "grid"),
            P("month", "grid", None, None, None),
            P("month", "grid", None),
        ),
        out_specs=P("month", "grid"),
        check_vma=False,
    )
```

time: 403 us -> 110 us (0.27); the launches traced: 399 us -> 110 us
  blocking collectives: 270 us -> 0 us
  Pallas kernels: 0 us -> 106 us
  matrix products: 74.1 us -> 0 us
  waiting for transfers between devices: 21 us -> 0 us
  starting transfers between devices: 18.4 us -> 0 us
  local copies, waits for them, and re-layouts: 10.3 us -> 3.71 us
  other arithmetic: 4.56 us -> 0 us
    all_gather x14 -> x0, blocking collectives: 211 us -> none  [local(): whole = lax.all_gather(apply_state, 'grid', axis=1, tiled=True)]
    pallas_call x0 -> x1, Pallas kernels: none -> 106 us  [local(): pl.pallas_call(functools.partial(kernel, sections, n, cap, months, nb, kk...]
    dot_general x14 -> x0, matrix products: 74.1 us -> none  [local(): jnp.einsum('tbkc,bkrc->tbr', picked, blocks[apply_month_idx], precision=l...]
    psum x4 -> x0, blocking collectives: 59.1 us -> none  [local(): inventory = lax.psum(jnp.sum(held, axis=1), 'grid')]
    ppermute x8 -> x0, waiting for transfers between devices: 21 us -> none  [passed_along(): lax.ppermute(value, axis, [(i, (i + by) % devices) for i in range(devices)])]
    ppermute x8 -> x0, starting transfers between devices: 18.4 us -> none  [passed_along(): lax.ppermute(value, axis, [(i, (i + by) % devices) for i in range(devices)])]
    gather x14 -> x0, local copies, waits for them, and re-layouts: 8.82 us -> none  [local(): picked = whole.reshape(batch, -1, blk_size)[:, cols[apply_month_idx]]]
  transfers between devices with their start and end apart: 8 -> 0, of which waited for: 8 -> 0; matrix products, arithmetic and copies ran while one was open for 0% -> 0% of each run, Pallas kernels for 0% -> 0%
where the time goes in v1:
time: 110 us
  Pallas kernels  106 us (96%)
  local copies, waits for them, and re-layouts  3.71 us (3%)
    pallas_call x1, Pallas kernels, local(): pl.pallas_call(functools.partial(kernel, sections, n, cap, months, nb, kk...  106 us
    unnamed x7, local copies, waits for them, and re-layouts  2.93 us

profile of v1, /device:TPU:6, one launch (start us, length us, event | category | flops | bytes accessed | tf_op | source)
XLA Modules:
  0.0 109.9 jit_solution(17871661234670589851)
XLA Ops:
  0.0 0.8 reshape.7.cols_s.cols_v
  0.8 0.0 copy-start
  0.8 0.9 copy-done
  1.7 0.0 copy-start.1
  1.7 0.7 copy-done.1
  2.4 0.0 copy-start.2
  2.4 0.7 copy-done.2
  3.1 106.2 %shard_map.55 = f32[16,1024]{1,0:T(8,128)S(1)} custom-call(f32[64,1024]{1,0:T(8,128)S(1)} %copy-done, f32[1,64]{1,0:T(1,128)S(1)} %bitcast.1, f32[2,1024]{1,0:T(2,128)S(1)} %copy-done.1, f32[2,8,8,128,128]{4,3,2,1,0:T(8,128)} %blocks.1, s32[1,128]{1,0:T(1,128)S(1)} %reshape.7.cols_s.cols_v, s32[1,128]{1,0:T(1,128)S(1)} %reshape.7.cols_s.cols_v), custom_call_target="tpu_custom_call" | custom-call | tf_op jit(solution)/shard_map/pallas_call | solution.py:292
  109.3 0.6 copy.7
Async XLA Ops:
  0.8 1.0 copy-start
  1.7 0.7 copy-start.1
  2.4 0.7 copy-start.2

commit v2 on v1

--- a/solution.py
+++ b/solution.py
@@ -9,17 +9,17 @@
 
 FAR = 2
 TB = 8
-NT = (((1,), (1,)), ((), ()))
 F32, BF16, I32 = jnp.float32, jnp.bfloat16, jnp.int32
 
 
 def kernel(
     sections, n, cap, months, nb, kk, bs, nbatch,
-    tracers, targets, retain, blocks, cols_s, cols_v,
+    tracers_h, targets_h, retain_h, blocks, cols_h,
     out,
+    tracers, targets, retain, cols_s,
     wf, whi, wlo, xin, xmid, xout, hl, cur, far, acc, sendbuf, recv, psend, precv, fout,
-    cstage, crecv, csmem, send_tab, pos_tab,
-    w_sem, c_send, c_recv, c_loc, h_send, h_recv, in_send, in_recv, p_send, p_recv, o_send, o_recv,
+    crecv, csmem, send_tab, pos_tab,
+    a_sem, w_sem, c_send, c_recv, c_loc, h_send, h_recv, in_send, in_recv, p_send, p_recv, o_send, o_recv,
 ):
     tb = TB
     near = kk - FAR
@@ -37,6 +37,14 @@
     def chunk(j, i):
         return pltpu.make_async_copy(blocks.at[j, i], wf.at[j, i], w_sem.at[j, i])
 
+    get_cols = pltpu.make_async_copy(cols_h, cols_s, a_sem.at[0])
+    get_tracers = pltpu.make_async_copy(tracers_h, tracers, a_sem.at[1])
+    get_retain = pltpu.make_async_copy(retain_h, retain, a_sem.at[2])
+    get_targets = pltpu.make_async_copy(targets_h, targets, a_sem.at[3])
+    get_cols.start()
+    get_tracers.start()
+    get_retain.start()
+    get_targets.start()
     for j in range(months):
         for i in range(nb):
             chunk(j, i).start()
@@ -48,14 +56,18 @@
         pl.semaphore_signal(
             barrier, inc=1, device_id={"month": lax.rem(s + o, sections)}, device_id_type=pl.DeviceIdType.MESH
         )
-    cstage[...] = jnp.broadcast_to(cols_v[...], cstage.shape)
     pl.semaphore_wait(barrier, n - 1 + sections - 1)
 
     for o in offsets:
         pltpu.make_async_remote_copy(
-            cstage, crecv.at[o - 1], c_send, c_recv,
+            cols_h, crecv.at[o - 1], c_send, c_recv,
             device_id={"grid": peer(o)}, device_id_type=pl.DeviceIdType.MESH,
         ).start()
+
+    get_cols.wait()
+    get_tracers.wait()
+    get_retain.wait()
+    get_targets.wait()
 
     @pl.when(s == 0)
     def _():
@@ -64,10 +76,10 @@
                 xin[b, i] = tracers[b * tb : (b + 1) * tb, i * bs : (i + 1) * bs]
 
     def far_at(j, e):
-        return j * nb * kk + (e // FAR) * kk + near + e % FAR
+        return j, e // FAR, near + e % FAR
 
     for j in range(months):
-        owners = [cols_s[0, far_at(j, e)] // nb for e in range(nfar)]
+        owners = [cols_s[far_at(j, e)] // nb for e in range(nfar)]
         for e in range(nfar):
             rank = I32(0)
             for f in range(e):
@@ -87,7 +99,7 @@
             count = I32(0)
             idx = [I32(0)] * cap
             for e in range(nfar):
-                c = csmem[n - 1 - o, 0, far_at(j, e)] - g * nb
+                c = csmem[(n - 1 - o,) + far_at(j, e)] - g * nb
                 hit = (c >= 0) & (c < nb)
                 for r in range(cap):
                     idx[r] = jnp.where(hit & (count == r), c, idx[r])
@@ -102,10 +114,10 @@
         def one(i, carry):
             chunk(j, i).wait()
             for k in range(kk):
-                b = wf[j, i, k]
+                b = wf[j, i, k].T
                 hi = b.astype(BF16)
-                whi[j, i, :, k * bs : (k + 1) * bs] = hi
-                wlo[j, i, :, k * bs : (k + 1) * bs] = (b - hi.astype(F32)).astype(BF16)
+                whi[j, i, k * bs : (k + 1) * bs, :] = hi
+                wlo[j, i, k * bs : (k + 1) * bs, :] = (b - hi.astype(F32)).astype(BF16)
             return carry
 
         lax.fori_loop(0, nb, one, 0)
@@ -115,8 +127,8 @@
         return jnp.concatenate([hi, v - hi], axis=0).astype(BF16)
 
     def product(rows, j, i, lo, hi):
-        d = lax.dot_general(rows, whi[j, i, :, lo * bs : hi * bs], NT, preferred_element_type=F32)
-        d = d + lax.dot_general(rows, wlo[j, i, :, lo * bs : hi * bs], NT, preferred_element_type=F32)
+        d = jnp.dot(rows, whi[j, i, lo * bs : hi * bs, :], preferred_element_type=F32)
+        d = d + jnp.dot(rows, wlo[j, i, lo * bs : hi * bs, :], preferred_element_type=F32)
         return d[:tb] + d[tb:]
 
     def send_halo(b, j, src):
@@ -140,7 +152,7 @@
         for i in range(nb):
             picked = [hl[i]]
             for k in range(1, near):
-                picked.append(hl[jnp.clip(cols_s[0, j * nb * kk + i * kk + k] - g * nb, 0, nb - 1)])
+                picked.append(hl[jnp.clip(cols_s[j, i, k] - g * nb, 0, nb - 1)])
             rows = jnp.concatenate(picked, axis=1)
             keep = retain[j : j + 1, i * bs : (i + 1) * bs]
             acc[i] = keep * src[b, i] + product(rows, j, i, 0, near)
@@ -286,23 +298,21 @@
         nbatch = count // TB
         cap = -(-nb * FAR // (n - 1))
         slots = (n - 1) * cap
-        flat = cols.reshape(1, -1)
         dma = pltpu.SemaphoreType.DMA
         vmem = pl.BlockSpec(memory_space=pltpu.VMEM)
         return pl.pallas_call(
             functools.partial(kernel, sections, n, cap, months, nb, kk, bs, nbatch),
             out_shape=jax.ShapeDtypeStruct((count // sections, rows), F32),
-            in_specs=[
-                vmem, vmem, vmem,
-                pl.BlockSpec(memory_space=pl.ANY),
-                pl.BlockSpec(memory_space=pltpu.SMEM),
-                vmem,
-            ],
+            in_specs=[pl.BlockSpec(memory_space=pltpu.HBM)] * 5,
             out_specs=vmem,
             scratch_shapes=[
+                pltpu.VMEM(tracers.shape, F32),
+                pltpu.VMEM((1, count), F32),
+                pltpu.VMEM(retain.shape, F32),
+                pltpu.SMEM(cols.shape, I32),
                 pltpu.VMEM((months, nb, kk, bs, bs), F32),
-                pltpu.VMEM((months, nb, bs, kk * bs), BF16),
-                pltpu.VMEM((months, nb, bs, kk * bs), BF16),
+                pltpu.VMEM((months, nb, kk * bs, bs), BF16),
+                pltpu.VMEM((months, nb, kk * bs, bs), BF16),
                 pltpu.VMEM((nbatch, nb, TB, bs), F32),
                 pltpu.VMEM((nbatch, nb, TB, bs), F32),
                 pltpu.VMEM((nbatch, nb, TB, bs), F32),
@@ -315,12 +325,11 @@
                 pltpu.VMEM((nbatch, TB, bs), F32),
                 pltpu.VMEM((nbatch, n - 1, TB, bs), F32),
                 pltpu.VMEM((nbatch, TB, rows), F32),
-                pltpu.VMEM((8, flat.shape[1]), I32),
-                pltpu.VMEM((n - 1, 8, flat.shape[1]), I32),
-                pltpu.SMEM((n - 1, 8, flat.shape[1]), I32),
+                pltpu.VMEM((n - 1,) + cols.shape, I32),
+                pltpu.SMEM((n - 1,) + cols.shape, I32),
                 pltpu.SMEM((months * slots,), I32),
                 pltpu.SMEM((months * nb * FAR,), I32),
-                dma((months, nb)),
+                dma((4,)), dma((months, nb)),
                 dma, dma, dma,
                 dma((nbatch, months)), dma((nbatch, months)),
                 dma((nbatch,)), dma((nbatch,)),
@@ -328,9 +337,9 @@
                 dma((nbatch,)), dma,
             ],
             compiler_params=pltpu.CompilerParams(
-                collective_id=0, has_side_effects=True, vmem_limit_bytes=48 * 1024 * 1024
+                collective_id=0, has_side_effects=True, vmem_limit_bytes=63 * 1024 * 1024 + 768 * 1024
             ),
-        )(tracers, targets.reshape(1, -1), retain, blocks, flat, flat)
+        )(tracers, targets.reshape(1, -1), retain, blocks, cols)
 
     return jax.shard_map(
         local,

time: 110 us -> 107 us (0.973)
  local copies, waits for them, and re-layouts: 3.71 us -> 1.47 us
    unnamed x7 -> x1, local copies, waits for them, and re-layouts: 2.93 us -> 1.47 us
    pallas_call x1, Pallas kernels: 106 us -> 105 us  [local(): pl.pallas_call(functools.partial(kernel, sections, n, cap, months, nb, kk...]
where the time goes in v2:
time: 107 us; the launch traced here: 106 us
  Pallas kernels  105 us (98%)
  local copies, waits for them, and re-layouts  1.47 us (1%)
    pallas_call x1, Pallas kernels, local(): pl.pallas_call(functools.partial(kernel, sections, n, cap, months, nb, kk...  105 us

profile of v2, /device:TPU:6, one launch (start us, length us, event | category | flops | bytes accessed | tf_op | source)
XLA Modules:
  0.0 106.4 jit_solution(16215560123714754594)
XLA Ops:
  0.0 104.9 %shard_map.55 = f32[16,1024]{1,0:T(8,128)} custom-call(f32[64,1024]{1,0:T(8,128)} %tracers_h.1, f32[1,64]{1,0:T(1,128)} %bitcast.1, f32[2,1024]{1,0:T(2,128)} %retain_h.1, f32[2,8,8,128,128]{4,3,2,1,0:T(8,128)} %blocks.1, s32[2,8,8]{2,1,0:T(8,128)} %cols_h.1), custom_call_target="tpu_custom_call" | custom-call | tf_op jit(solution)/shard_map/pallas_call | solution.py:303
  104.9 1.5 %copy.7 = f32[16,1024]{1,0:T(8,128)} copy(f32[16,1024]{1,0:T(8,128)} %shard_map.55) | data formatting | bytes 131072

commit v3 on v2

--- a/solution.py
+++ b/solution.py
@@ -8,7 +8,7 @@
 from jax.sharding import PartitionSpec as P
 
 FAR = 2
-TB = 8
+TB = 16
 F32, BF16, I32 = jnp.float32, jnp.bfloat16, jnp.int32
 
 

time: 107 us -> 112 us (1.047)
  Pallas kernels: 105 us -> 110 us
    pallas_call x1, Pallas kernels: 105 us -> 110 us  [local(): pl.pallas_call(functools.partial(kernel, sections, n, cap, months, nb, kk...]
where the time goes in v3:
time: 112 us
  Pallas kernels  110 us (98%)
  local copies, waits for them, and re-layouts  1.47 us (1%)
    pallas_call x1, Pallas kernels, local(): pl.pallas_call(functools.partial(kernel, sections, n, cap, months, nb, kk...  110 us

profile of v3, /device:TPU:6, one launch (start us, length us, event | category | flops | bytes accessed | tf_op | source)
XLA Modules:
  0.0 111.6 jit_solution(7484814874460250761)
XLA Ops:
  0.0 110.1 %shard_map.55 = f32[16,1024]{1,0:T(8,128)} custom-call(f32[64,1024]{1,0:T(8,128)} %tracers_h.1, f32[1,64]{1,0:T(1,128)} %bitcast.1, f32[2,1024]{1,0:T(2,128)} %retain_h.1, f32[2,8,8,128,128]{4,3,2,1,0:T(8,128)} %blocks.1, s32[2,8,8]{2,1,0:T(8,128)} %cols_h.1), custom_call_target="tpu_custom_call" | custom-call | tf_op jit(solution)/shard_map/pallas_call | solution.py:303
  110.1 1.5 %copy.7 = f32[16,1024]{1,0:T(8,128)} copy(f32[16,1024]{1,0:T(8,128)} %shard_map.55) | data formatting | bytes 131072

commit v4 on v2

--- a/solution.py
+++ b/solution.py
@@ -50,19 +50,22 @@
             chunk(j, i).start()
 
     barrier = pltpu.get_barrier_semaphore()
-    for o in range(1, n):
-        pl.semaphore_signal(barrier, inc=1, device_id={"grid": peer(o)}, device_id_type=pl.DeviceIdType.MESH)
-    for o in range(1, sections):
-        pl.semaphore_signal(
-            barrier, inc=1, device_id={"month": lax.rem(s + o, sections)}, device_id_type=pl.DeviceIdType.MESH
-        )
-    pl.semaphore_wait(barrier, n - 1 + sections - 1)
+    for d in range(sections):
+        for o in range(n):
+            if d + o > 0:
+                pl.semaphore_signal(
+                    barrier, inc=1, device_id={"month": lax.rem(s + d, sections), "grid": peer(o)},
+                    device_id_type=pl.DeviceIdType.MESH,
+                )
+    pl.semaphore_wait(barrier, n * sections - 1)
 
     for o in offsets:
-        pltpu.make_async_remote_copy(
-            cols_h, crecv.at[o - 1], c_send, c_recv,
-            device_id={"grid": peer(o)}, device_id_type=pl.DeviceIdType.MESH,
-        ).start()
+        for group in range(2):
+            pltpu.make_async_remote_copy(
+                cols_h, crecv.at[group, o - 1], c_send, c_recv,
+                device_id={"month": lax.rem(s + group * (sections - 1), sections), "grid": peer(o)},
+                device_id_type=pl.DeviceIdType.MESH,
+            ).start()
 
     get_cols.wait()
     get_tracers.wait()
@@ -99,7 +102,7 @@
             count = I32(0)
             idx = [I32(0)] * cap
             for e in range(nfar):
-                c = csmem[(n - 1 - o,) + far_at(j, e)] - g * nb
+                c = csmem[(1 - j, n - 1 - o) + far_at(j, e)] - g * nb
                 hit = (c >= 0) & (c < nb)
                 for r in range(cap):
                     idx[r] = jnp.where(hit & (count == r), c, idx[r])
@@ -131,9 +134,10 @@
         d = d + jnp.dot(rows, wlo[j, i, lo * bs : hi * bs, :], preferred_element_type=F32)
         return d[:tb] + d[tb:]
 
-    def send_halo(b, j, src):
-        for i in range(nb):
-            cur[i] = src[b, i]
+    def send_halo(b, j, part):
+        for i in range(nb):
+            cur[i] = part(i)
+        goal = lax.rem(s + 1 - j, sections)
         for o in offsets:
             for r in range(cap):
                 q = (o - 1) * cap + r
@@ -143,7 +147,7 @@
                 sendbuf.at[b, j, pl.ds((o - 1) * cap, cap)],
                 recv.at[b, j, pl.ds((o - 1) * cap, cap)],
                 h_send.at[b, j], h_recv.at[b, j],
-                device_id={"grid": peer(o)}, device_id_type=pl.DeviceIdType.MESH,
+                device_id={"month": goal, "grid": peer(o)}, device_id_type=pl.DeviceIdType.MESH,
             ).start()
 
     def apply(b, j, src, dst):
@@ -163,16 +167,13 @@
             rows = jnp.concatenate([far[pos_tab[j * nfar + i * FAR + f]] for f in range(FAR)], axis=1)
             dst[b, i] = acc[i] + product(rows, j, i, near, kk)
 
-    def enter(b):
+    def middle(b):
         @pl.when(s > 0)
         def _():
             pltpu.make_async_copy(xin.at[b], xin.at[b], in_recv.at[b]).wait()
 
-        send_halo(b, 0, xin)
-
-    def middle(b):
         apply(b, 0, xin, xmid)
-        send_halo(b, 1, xmid)
+        send_halo(b, 1, lambda i: xmid[b, i])
 
     def passed(b):
         return pltpu.make_async_remote_copy(
@@ -186,6 +187,7 @@
         @pl.when(s < last)
         def _():
             passed(b).start()
+            send_halo(b, 0, lambda i: xout[b, i])
 
         @pl.when(s == last)
         def _():
@@ -232,34 +234,41 @@
 
     make_table(0)
 
+    @pl.when(s == last)
+    def _():
+        def one(b, carry):
+            at = pl.multiple_of(b * tb, tb)
+            send_halo(b, 0, lambda i: tracers[pl.ds(at, tb), i * bs : (i + 1) * bs])
+            return carry
+
+        lax.fori_loop(0, nbatch, one, 0)
+
+    make_table(1)
+    prep(0)
+
+    @pl.when(s > 0)
+    def _():
+        prep(1)
+
+    middle(I32(0))
+
     @pl.when(s == 0)
     def _():
-        enter(I32(0))
-        make_table(1)
-        prep(0)
-
-    @pl.when(s > 0)
-    def _():
-        make_table(1)
-        prep(0)
         prep(1)
-        enter(I32(0))
-
-    middle(I32(0))
-
-    @pl.when(s == 0)
-    def _():
-        prep(1)
 
     def step(b, carry):
-        enter(b)
+        middle(b)
+
+        @pl.when(b >= 2)
+        def _():
+            finish(b - 2)
+
         leave(b - 1)
-        middle(b)
-        finish(b - 1)
         return carry
 
     lax.fori_loop(1, nbatch, step, 0)
     leave(I32(nbatch - 1))
+    finish(I32(nbatch - 2))
     finish(I32(nbatch - 1))
 
     pltpu.make_async_copy(crecv, crecv, c_send).wait()
@@ -325,8 +334,8 @@
                 pltpu.VMEM((nbatch, TB, bs), F32),
                 pltpu.VMEM((nbatch, n - 1, TB, bs), F32),
                 pltpu.VMEM((nbatch, TB, rows), F32),
-                pltpu.VMEM((n - 1,) + cols.shape, I32),
-                pltpu.SMEM((n - 1,) + cols.shape, I32),
+                pltpu.VMEM((2, n - 1) + cols.shape, I32),
+                pltpu.SMEM((2, n - 1) + cols.shape, I32),
                 pltpu.SMEM((months * slots,), I32),
                 pltpu.SMEM((months * nb * FAR,), I32),
                 dma((4,)), dma((months, nb)),

time: 107 us -> 105 us (0.981)
  Pallas kernels: 105 us -> 103 us
    pallas_call x1, Pallas kernels: 105 us -> 103 us  [local(): pl.pallas_call(functools.partial(kernel, sections, n, cap, months, nb, kk...]
where the time goes in v4:
time: 105 us
  Pallas kernels  103 us (98%)
  local copies, waits for them, and re-layouts  1.47 us (1%)
    pallas_call x1, Pallas kernels, local(): pl.pallas_call(functools.partial(kernel, sections, n, cap, months, nb, kk...  103 us

profile of v4, /device:TPU:6, one launch (start us, length us, event | category | flops | bytes accessed | tf_op | source)
XLA Modules:
  0.0 104.8 jit_solution(477293859768402226)
XLA Ops:
  0.0 103.3 %shard_map.55 = f32[16,1024]{1,0:T(8,128)} custom-call(f32[64,1024]{1,0:T(8,128)} %tracers_h.1, f32[1,64]{1,0:T(1,128)} %bitcast.1, f32[2,1024]{1,0:T(2,128)} %retain_h.1, f32[2,8,8,128,128]{4,3,2,1,0:T(8,128)} %blocks.1, s32[2,8,8]{2,1,0:T(8,128)} %cols_h.1), custom_call_target="tpu_custom_call" | custom-call | tf_op jit(solution)/shard_map/pallas_call | solution.py:312
  103.3 1.5 %copy.7 = f32[16,1024]{1,0:T(8,128)} copy(f32[16,1024]{1,0:T(8,128)} %shard_map.55) | data formatting | bytes 131072

commit v5 on v4

--- a/solution.py
+++ b/solution.py
@@ -96,19 +96,19 @@
     local.start()
     local.wait()
 
-    def make_table(j):
+    def make_table(t, group, j):
         def one(q, carry):
             o = q + 1
             count = I32(0)
             idx = [I32(0)] * cap
             for e in range(nfar):
-                c = csmem[(1 - j, n - 1 - o) + far_at(j, e)] - g * nb
+                c = csmem[(group, n - 1 - o) + far_at(j, e)] - g * nb
                 hit = (c >= 0) & (c < nb)
                 for r in range(cap):
                     idx[r] = jnp.where(hit & (count == r), c, idx[r])
                 count = count + jnp.where(hit, 1, 0)
             for r in range(cap):
-                send_tab[(j * (n - 1) + q) * cap + r] = idx[r]
+                send_tab[(t * (n - 1) + q) * cap + r] = idx[r]
             return carry
 
         lax.fori_loop(0, n - 1, one, 0)
@@ -134,19 +134,20 @@
         d = d + jnp.dot(rows, wlo[j, i, lo * bs : hi * bs, :], preferred_element_type=F32)
         return d[:tb] + d[tb:]
 
-    def send_halo(b, j, part):
+    def send_halo(b, t, part):
         for i in range(nb):
             cur[i] = part(i)
-        goal = lax.rem(s + 1 - j, sections)
+        j = t % 2
+        goal = lax.rem(s + (t == 0), sections)
         for o in offsets:
             for r in range(cap):
                 q = (o - 1) * cap + r
-                idx = send_tab[j * (n - 1) * cap + q]
-                sendbuf[b, j, q] = cur[idx]
+                idx = send_tab[t * (n - 1) * cap + q]
+                sendbuf[b, t, q] = cur[idx]
             pltpu.make_async_remote_copy(
-                sendbuf.at[b, j, pl.ds((o - 1) * cap, cap)],
+                sendbuf.at[b, t, pl.ds((o - 1) * cap, cap)],
                 recv.at[b, j, pl.ds((o - 1) * cap, cap)],
-                h_send.at[b, j], h_recv.at[b, j],
+                h_send.at[b, t], h_recv.at[b, j],
                 device_id={"month": goal, "grid": peer(o)}, device_id_type=pl.DeviceIdType.MESH,
             ).start()
 
@@ -232,18 +233,17 @@
                 at = pl.multiple_of(lax.rem(b, per) * tb, tb)
                 out[pl.ds(at, tb), :] = fout[b]
 
-    make_table(0)
-
-    @pl.when(s == last)
-    def _():
-        def one(b, carry):
-            at = pl.multiple_of(b * tb, tb)
-            send_halo(b, 0, lambda i: tracers[pl.ds(at, tb), i * bs : (i + 1) * bs])
-            return carry
-
-        lax.fori_loop(0, nbatch, one, 0)
-
-    make_table(1)
+    def first(b):
+        at = pl.multiple_of(b * tb, tb)
+        send_halo(b, 2, lambda i: tracers[pl.ds(at, tb), i * bs : (i + 1) * bs])
+
+    @pl.when(s == 0)
+    def _():
+        make_table(2, 0, 0)
+        first(I32(0))
+
+    make_table(0, 1, 0)
+    make_table(1, 0, 1)
     prep(0)
 
     @pl.when(s > 0)
@@ -254,10 +254,15 @@
 
     @pl.when(s == 0)
     def _():
+        first(I32(1))
         prep(1)
 
     def step(b, carry):
         middle(b)
+
+        @pl.when((s == 0) & (b < nbatch - 1))
+        def _():
+            first(b + 1)
 
         @pl.when(b >= 2)
         def _():
@@ -274,8 +279,18 @@
     pltpu.make_async_copy(crecv, crecv, c_send).wait()
 
     def drain(b, carry):
-        for j in range(months):
-            pltpu.make_async_copy(sendbuf.at[b, j], sendbuf.at[b, j], h_send.at[b, j]).wait()
+        def sent(t):
+            pltpu.make_async_copy(sendbuf.at[b, t], sendbuf.at[b, t], h_send.at[b, t]).wait()
+
+        sent(1)
+
+        @pl.when(s < last)
+        def _():
+            sent(0)
+
+        @pl.when(s == 0)
+        def _():
+            sent(2)
 
         @pl.when(s < last)
         def _():
@@ -329,18 +344,18 @@
                 pltpu.VMEM((nb, TB, bs), F32),
                 pltpu.VMEM((slots, 2 * TB, bs), BF16),
                 pltpu.VMEM((nb, TB, bs), F32),
-                pltpu.VMEM((nbatch, months, slots, TB, bs), F32),
+                pltpu.VMEM((nbatch, 3, slots, TB, bs), F32),
                 pltpu.VMEM((nbatch, months, slots, TB, bs), F32),
                 pltpu.VMEM((nbatch, TB, bs), F32),
                 pltpu.VMEM((nbatch, n - 1, TB, bs), F32),
                 pltpu.VMEM((nbatch, TB, rows), F32),
                 pltpu.VMEM((2, n - 1) + cols.shape, I32),
                 pltpu.SMEM((2, n - 1) + cols.shape, I32),
-                pltpu.SMEM((months * slots,), I32),
+                pltpu.SMEM((3 * slots,), I32),
                 pltpu.SMEM((months * nb * FAR,), I32),
                 dma((4,)), dma((months, nb)),
                 dma, dma, dma,
-                dma((nbatch, months)), dma((nbatch, months)),
+                dma((nbatch, 3)), dma((nbatch, months)),
                 dma((nbatch,)), dma((nbatch,)),
                 dma((nbatch,)), dma((nbatch,)),
                 dma((nbatch,)), dma,

time: 105 us -> 114 us (1.086)
  Pallas kernels: 103 us -> 113 us
    pallas_call x1, Pallas kernels: 103 us -> 113 us  [local(): pl.pallas_call(functools.partial(kernel, sections, n, cap, months, nb, kk...]
where the time goes in v5:
time: 114 us
  Pallas kernels  113 us (99%)
  local copies, waits for them, and re-layouts  1.47 us (1%)
    pallas_call x1, Pallas kernels, local(): pl.pallas_call(functools.partial(kernel, sections, n, cap, months, nb, kk...  113 us

profile of v5, /device:TPU:6, one launch (start us, length us, event | category | flops | bytes accessed | tf_op | source)
XLA Modules:
  0.0 114.3 jit_solution(15918903359723434527)
XLA Ops:
  0.0 112.8 %shard_map.55 = f32[16,1024]{1,0:T(8,128)} custom-call(f32[64,1024]{1,0:T(8,128)} %tracers_h.1, f32[1,64]{1,0:T(1,128)} %bitcast.1, f32[2,1024]{1,0:T(2,128)} %retain_h.1, f32[2,8,8,128,128]{4,3,2,1,0:T(8,128)} %blocks.1, s32[2,8,8]{2,1,0:T(8,128)} %cols_h.1), custom_call_target="tpu_custom_call" | custom-call | tf_op jit(solution)/shard_map/pallas_call | solution.py:327
  112.8 1.5 %copy.7 = f32[16,1024]{1,0:T(8,128)} copy(f32[16,1024]{1,0:T(8,128)} %shard_map.55) | data formatting | bytes 131072
